TPU v7x, 32 devices: a whole 2x2x4 slice. The times are simulated.
32 devices in a mesh: tok: 8 (over z, core), mdl: 4 (over y, x).
Axes of the slice: x: 2, y: 2, z: 4, core: 2. Of those that a mesh axis runs over, the one named last changes fastest.
Arguments:
- hidden_in: bfloat16 [8, 2228224], P('tok', 'mdl'), may hold values from -6 to 6
- doc_ids: int32 [16384], P('tok'), may hold values from 0 to 2, as said below
- ln1_gain: float32 [1088], replicated, may hold values from 0.25 to 1.75
- ln1_bias: float32 [1088], replicated, may hold values from -3 to 3
- w_qkv: bfloat16 [1088, 3264], P('tok', 'mdl'), may hold values from -0.25 to 0.25
- q_bias: float32 [1088], replicated, may hold values from -3 to 3
- v_bias: float32 [1088], replicated, may hold values from -3 to 3
- w_out: bfloat16 [1088, 1088], P('tok', 'mdl'), may hold values from -1 to 1
- out_bias: float32 [1088], replicated, may hold values from -3 to 3
- ln2_gain: float32 [1088], replicated, may hold values from 0.25 to 1.75
- ln2_bias: float32 [1088], replicated, may hold values from -3 to 3
- w_fc1: bfloat16 [1088, 4352], P('tok', 'mdl'), may hold values from -0.1875 to 0.1875
- fc1_bias: float32 [4352], replicated, may hold values from -3 to 3
- w_fc2: bfloat16 [4352, 1088], P('tok', 'mdl'), may hold values from -0.09375 to 0.09375
- fc2_bias: float32 [1088], replicated, may hold values from -3 to 3
- cotangent: bfloat16 [8, 2228224], P('tok', 'mdl'), may hold values from -6 to 6
Outputs:
- result: bfloat16 [8, 2228224], P('tok', 'mdl')
- input_grad: bfloat16 [8, 2228224], P('tok', 'mdl')
- w_qkv_grad: float32 [1088, 3264], P('tok', 'mdl')
- w_out_grad: float32 [1088, 1088], P('tok', 'mdl')
- w_fc1_grad: float32 [1088, 4352], P('tok', 'mdl')
- w_fc2_grad: float32 [4352, 1088], P('tok', 'mdl')
- ln1_gain_grad: float32 [1088], replicated
- ln1_bias_grad: float32 [1088], replicated
- q_bias_grad: float32 [1088], replicated
- v_bias_grad: float32 [1088], replicated
- out_bias_grad: float32 [1088], replicated
- ln2_gain_grad: float32 [1088], replicated
- ln2_bias_grad: float32 [1088], replicated
- fc1_bias_grad: float32 [4352], replicated
- fc2_bias_grad: float32 [1088], replicated
Inputs may be any that keep to these rules, and one draw needn't show every extreme that they name: `doc_ids`: every window of 2048 tokens holds exactly three documents numbered 0, 1, 2 in token order; document 0 ends within the window's first 512 tokens and document 2 starts within its last 512 tokens.
All inputs are finite; a program needn't handle non-finite values.
Results may differ from a plain program's by a relative error of at most 0.017.
Values may be sent and summed in bfloat16 or wider, within the bound.
A program may use at most 448 MiB of HBM per device.

v0:
```python
import jax
import jax.numpy as jnp
from jax import lax
from jax.sharding import PartitionSpec as P

D = 1088
HEADS = 17
HEAD_DIM = 64
SEQ = 2048


EPSILON = 1e-05
SCORE_SCALE = 0.125
MASKED = -1e30


def normalize(values, gain_vec, shift_vec):
    centered = values - jnp.mean(values, axis=-1, keepdims=True)
    inv_root = lax.rsqrt(jnp.mean(centered * centered, axis=-1, keepdims=True) + EPSILON)
    scaled = centered * inv_root
    return (scaled * gain_vec + shift_vec, scaled, inv_root)


def normalize_back(gradient, scaled, inv_root, gain_vec):
    weighted = gradient * gain_vec
    inner = (
        weighted
        - jnp.mean(weighted, axis=-1, keepdims=True)
        - scaled * jnp.mean(weighted * scaled, axis=-1, keepdims=True)
    )
    return (inv_root * inner, jnp.sum(gradient * scaled, axis=0), jnp.sum(gradient, axis=0))


def body(
    hidden_in,
    doc_ids,
    ln1_gain,
    ln1_bias,
    w_qkv,
    q_bias,
    v_bias,
    w_out,
    out_bias,
    ln2_gain,
    ln2_bias,
    w_fc1,
    fc1_bias,
    w_fc2,
    fc2_bias,
    cotangent,
):
    my_group = lax.axis_index("mdl")
    windows = hidden_in.shape[0]
    piece_len = hidden_in.shape[1] // D
    row_total = windows * piece_len
    input_rows = hidden_in.reshape(row_total, D).astype(jnp.float32)
    cot_low = cotangent.reshape(row_total, D)
    cot_rows = cot_low.astype(jnp.float32)
    column_weights = (
        lax.all_gather(w_qkv, "tok", axis=0, tiled=True),
        lax.all_gather(w_out, "tok", axis=0, tiled=True),
        lax.all_gather(w_fc1, "tok", axis=0, tiled=True),
        lax.all_gather(w_fc2, "tok", axis=0, tiled=True),
    )

    def project(inputs, matrix_index):
        gathered = lax.all_gather(inputs, "mdl", axis=0, tiled=True)
        partial_out = jnp.dot(
            gathered, column_weights[matrix_index], preferred_element_type=jnp.float32
        )
        product = lax.all_to_all(partial_out, "mdl", split_axis=0, concat_axis=1, tiled=True)
        return (product, gathered)

    def project_back(kept_input, gradient, matrix_index):
        grad_cols = lax.all_to_all(gradient, "mdl", split_axis=1, concat_axis=0, tiled=True)
        weight_grad = jnp.einsum(
            "ri,rc->ic", kept_input, grad_cols, preferred_element_type=jnp.float32
        )
        back_grad = lax.psum_scatter(
            jnp.einsum(
                "rc,ic->ri",
                grad_cols,
                column_weights[matrix_index],
                preferred_element_type=jnp.float32,
            ),
            "mdl",
            scatter_dimension=0,
            tiled=True,
        )
        return (back_grad, weight_grad)

    query_pos = my_group * piece_len + jnp.arange(piece_len)
    key_pos = jnp.arange(SEQ)
    doc_windows = doc_ids.reshape(windows, SEQ)

    def window_scores(query_heads, key_heads, doc_block):
        own_docs = lax.dynamic_slice_in_dim(doc_block, my_group * piece_len, piece_len, 0)
        visible = (own_docs[:, None] == doc_block[None, :]) & (
            key_pos[None, :] <= query_pos[:, None]
        )
        raw_scores = (
            jnp.einsum("qhd,khd->hqk", query_heads, key_heads, preferred_element_type=jnp.float32)
            * SCORE_SCALE
        )
        return jnp.where(visible[None], raw_scores, MASKED)

    first_out, scaled_one, inv_one = normalize(input_rows, ln1_gain, ln1_bias)
    first_norm = first_out.astype(jnp.bfloat16)
    qkv_product, kept_qkv = project(first_norm, 0)
    qkv = qkv_product + jnp.concatenate([q_bias, jnp.zeros((D,), jnp.float32), v_bias])
    queries = qkv[:, :D].astype(jnp.bfloat16)
    key_rows = qkv[:, D : 2 * D].astype(jnp.bfloat16)
    value_rows = qkv[:, 2 * D :].astype(jnp.bfloat16)
    key_local = key_rows.reshape(windows, 1, piece_len, D)
    value_local = value_rows.reshape(windows, 1, piece_len, D)
    query_windows = queries.reshape(windows, piece_len, D)
    key_all, value_all = (
        lax.all_gather(key_local, "mdl", axis=1, tiled=True),
        lax.all_gather(value_local, "mdl", axis=1, tiled=True),
    )

    def attend(loop_state, window_items):
        query_block, key_block, value_block, doc_block = window_items
        query_heads = query_block.reshape(piece_len, HEADS, HEAD_DIM)
        key_heads = key_block.reshape(SEQ, HEADS, HEAD_DIM)
        value_heads = value_block.reshape(SEQ, HEADS, HEAD_DIM)
        scores = window_scores(query_heads, key_heads, doc_block)
        top_score = jnp.max(scores, axis=-1, keepdims=True)
        weights_raw = jnp.exp(scores - top_score)
        row_total_w = jnp.sum(weights_raw, axis=-1, keepdims=True)
        probs = (weights_raw / row_total_w).astype(jnp.bfloat16)
        attended = jnp.einsum(
            "hqk,khd->qhd", probs, value_heads, preferred_element_type=jnp.float32
        )
        log_total = (top_score + jnp.log(row_total_w))[..., 0]
        return (loop_state, (attended.reshape(piece_len, D), log_total))

    unused_state, (attn_windows, log_totals) = lax.scan(
        attend, jnp.zeros((), jnp.float32), (query_windows, key_all, value_all, doc_windows)
    )
    attn_rows = attn_windows.reshape(row_total, D).astype(jnp.bfloat16)
    out_product, kept_out = project(attn_rows, 1)
    middle = input_rows + out_product + out_bias
    second_out, scaled_two, inv_two = normalize(middle, ln2_gain, ln2_bias)
    second_norm = second_out.astype(jnp.bfloat16)
    fc1_product, kept_fc1 = project(second_norm, 2)
    pre = fc1_product + fc1_bias
    activation = jax.nn.gelu(pre).astype(jnp.bfloat16)
    fc2_product, kept_fc2 = project(activation, 3)
    output_rows = middle + fc2_product + fc2_bias
    d_activation, grad_fc2 = project_back(kept_fc2, cot_low, 3)
    fc2_bias_grad = jnp.sum(cot_rows, axis=0)
    unused_value, gelu_back = jax.vjp(jax.nn.gelu, pre)
    d_pre = gelu_back(d_activation)[0]
    fc1_bias_grad = jnp.sum(d_pre, axis=0)
    d_second, grad_fc1 = project_back(kept_fc1, d_pre.astype(jnp.bfloat16), 2)
    d_middle_norm, ln2_gain_grad, ln2_bias_grad = normalize_back(
        d_second, scaled_two, inv_two, ln2_gain
    )
    d_middle = cot_rows + d_middle_norm
    out_bias_grad = jnp.sum(d_middle, axis=0)
    d_attn_rows, grad_out = project_back(kept_out, d_middle.astype(jnp.bfloat16), 1)
    d_attn_windows = d_attn_rows.astype(jnp.bfloat16).reshape(windows, piece_len, D)
    key_again, value_again = (
        lax.all_gather(key_local, "mdl", axis=1, tiled=True),
        lax.all_gather(value_local, "mdl", axis=1, tiled=True),
    )

    def attend_back(loop_state, window_items):
        query_block, key_block, value_block, grad_block, log_total, doc_block = window_items
        query_heads = query_block.reshape(piece_len, HEADS, HEAD_DIM)
        key_heads = key_block.reshape(SEQ, HEADS, HEAD_DIM)
        value_heads = value_block.reshape(SEQ, HEADS, HEAD_DIM)
        grad_heads = grad_block.reshape(piece_len, HEADS, HEAD_DIM)
        scores = window_scores(query_heads, key_heads, doc_block)
        probs = jnp.exp(scores - log_total[..., None])
        d_probs = jnp.einsum(
            "qhd,khd->hqk", grad_heads, value_heads, preferred_element_type=jnp.float32
        )
        centre = jnp.sum(probs * d_probs, axis=-1, keepdims=True)
        d_scores = (probs * (d_probs - centre)).astype(jnp.bfloat16)
        d_query = (
            jnp.einsum("hqk,khd->qhd", d_scores, key_heads, preferred_element_type=jnp.float32)
            * SCORE_SCALE
        )
        return (loop_state, (d_query.reshape(piece_len, D), centre[..., 0]))

    unused_back, back_outputs = lax.scan(
        attend_back,
        jnp.zeros((), jnp.float32),
        (query_windows, key_again, value_again, d_attn_windows, log_totals, doc_windows),
    )
    d_query_windows = back_outputs[0]
    centres = back_outputs[1]
    query_every, grad_every = (
        lax.all_gather(query_windows.reshape(windows, 1, piece_len, D), "mdl", axis=1, tiled=True),
        lax.all_gather(d_attn_windows.reshape(windows, 1, piece_len, D), "mdl", axis=1, tiled=True),
    )
    total_every, centre_every = (
        lax.all_gather(log_totals.reshape(windows, 1, HEADS, piece_len), "mdl", axis=1, tiled=True),
        lax.all_gather(centres.reshape(windows, 1, HEADS, piece_len), "mdl", axis=1, tiled=True),
    )
    own_pos = my_group * piece_len + jnp.arange(piece_len)

    def own_key_back(loop_state, window_items):
        key_block, value_block, query_block, grad_block, total_block, centre_block, doc_block = (
            window_items
        )
        key_heads = key_block.reshape(piece_len, HEADS, HEAD_DIM)
        value_heads = value_block.reshape(piece_len, HEADS, HEAD_DIM)
        query_heads = query_block.reshape(SEQ, HEADS, HEAD_DIM)
        grad_heads = grad_block.reshape(SEQ, HEADS, HEAD_DIM)
        total_rows = jnp.moveaxis(total_block, 0, 1).reshape(HEADS, SEQ)
        centre_rows = jnp.moveaxis(centre_block, 0, 1).reshape(HEADS, SEQ)
        own_docs = lax.dynamic_slice_in_dim(doc_block, my_group * piece_len, piece_len, 0)
        visible = (doc_block[:, None] == own_docs[None, :]) & (own_pos[None, :] <= key_pos[:, None])
        raw_scores = (
            jnp.einsum("qhd,khd->hqk", query_heads, key_heads, preferred_element_type=jnp.float32)
            * SCORE_SCALE
        )
        scores = jnp.where(visible[None], raw_scores, MASKED)
        probs = jnp.exp(scores - total_rows[..., None])
        d_probs = jnp.einsum(
            "qhd,khd->hqk", grad_heads, value_heads, preferred_element_type=jnp.float32
        )
        d_scores = (probs * (d_probs - centre_rows[..., None])).astype(jnp.bfloat16)
        d_key = (
            jnp.einsum("hqk,qhd->khd", d_scores, query_heads, preferred_element_type=jnp.float32)
            * SCORE_SCALE
        )
        d_value = jnp.einsum(
            "hqk,qhd->khd",
            probs.astype(jnp.bfloat16),
            grad_heads,
            preferred_element_type=jnp.float32,
        )
        return (
            loop_state,
            jnp.concatenate([d_key.reshape(piece_len, D), d_value.reshape(piece_len, D)], axis=-1),
        )

    unused_own, key_value_windows = lax.scan(
        own_key_back,
        jnp.zeros((), jnp.float32),
        (
            key_local[:, 0],
            value_local[:, 0],
            query_every,
            grad_every,
            total_every,
            centre_every,
            doc_windows,
        ),
    )
    key_value_mine = key_value_windows.reshape(row_total, 2 * D)
    d_qkv = jnp.concatenate([d_query_windows.reshape(row_total, D), key_value_mine], axis=-1)
    q_bias_grad = jnp.sum(d_qkv[:, :D], axis=0)
    v_bias_grad = jnp.sum(d_qkv[:, 2 * D :], axis=0)
    d_first, grad_qkv = project_back(kept_qkv, d_qkv.astype(jnp.bfloat16), 0)
    d_input_norm, ln1_gain_grad, ln1_bias_grad = normalize_back(
        d_first, scaled_one, inv_one, ln1_gain
    )
    d_input = d_middle + d_input_norm
    result = output_rows.astype(jnp.bfloat16).reshape(windows, piece_len * D)
    input_grad = d_input.astype(jnp.bfloat16).reshape(windows, piece_len * D)
    small_sums = lax.psum(
        (
            ln1_gain_grad,
            ln1_bias_grad,
            q_bias_grad,
            v_bias_grad,
            out_bias_grad,
            ln2_gain_grad,
            ln2_bias_grad,
            fc1_bias_grad,
            fc2_bias_grad,
        ),
        ("tok", "mdl"),
    )
    weight_parts = (grad_qkv, grad_out, grad_fc1, grad_fc2)
    weight_grads = (
        lax.psum_scatter(
            weight_parts[0].astype(jnp.bfloat16), "tok", scatter_dimension=0, tiled=True
        ).astype(jnp.float32),
        lax.psum_scatter(
            weight_parts[1].astype(jnp.bfloat16), "tok", scatter_dimension=0, tiled=True
        ).astype(jnp.float32),
        lax.psum_scatter(
            weight_parts[2].astype(jnp.bfloat16), "tok", scatter_dimension=0, tiled=True
        ).astype(jnp.float32),
        lax.psum_scatter(
            weight_parts[3].astype(jnp.bfloat16), "tok", scatter_dimension=0, tiled=True
        ).astype(jnp.float32),
    )
    return (
        result,
        input_grad,
        weight_grads[0],
        weight_grads[1],
        weight_grads[2],
        weight_grads[3],
        small_sums[0],
        small_sums[1],
        small_sums[2],
        small_sums[3],
        small_sums[4],
        small_sums[5],
        small_sums[6],
        small_sums[7],
        small_sums[8],
    )


def solution(mesh):
    in_specs = (
        P("tok", "mdl"),
        P("tok"),
        P(),
        P(),
        P("tok", "mdl"),
        P(),
        P(),
        P("tok", "mdl"),
        P(),
        P(),
        P(),
        P("tok", "mdl"),
        P(),
        P("tok", "mdl"),
        P(),
        P("tok", "mdl"),
    )
    out_specs = (
        P("tok", "mdl"),
        P("tok", "mdl"),
        P("tok", "mdl"),
        P("tok", "mdl"),
        P("tok", "mdl"),
        P("tok", "mdl"),
        P(),
        P(),
        P(),
        P(),
        P(),
        P(),
        P(),
        P(),
        P(),
    )
    return jax.shard_map(body, mesh=mesh, in_specs=in_specs, out_specs=out_specs, check_vma=False)
```

profile of v0, /device:TPU:0, one launch (start us, length us, event | category | flops | bytes accessed | tf_op | source)
XLA Modules:
  0.0 1930.9 jit_solution(5871893781699518629)
XLA Ops:
  8.0 21.9 %convert_reduce_fusion.1 = f32[557056]{0:T(1024)S(1)} fusion(bf16[1,557056]{1,0:T(2,128)(2,1)} %param.16), kind=kLoop, calls=%fused_computation.88 | loop fusion | flops 557056 | bytes 3342336 | tf_op jit(solution)/shard_map/convert_element_type | solution.py:56
  40.3 56.7 %all-gather.21.cloned.1.call-done = bf16[2048,1088]{0,1:T(8,128)(2,1)} async-done(((bf16[512,1088]{0,1:T(8,128)(2,1)}), bf16[2048,1088]{0,1:T(8,128)(2,1)}) %all-gather.21.cloned.1.call-update) | async-done | bytes 4456464 | tf_op jit(solution)/shard_map/all_gather | solution.py:67
  113.3 74.2 %all-to-all-done = f32[4,512,816]{1,2,0:T(8,128)} async-done(((f32[4,512,816]{1,2,0:T(8,128)}), f32[4,512,816]{1,2,0:T(8,128)}, u32[]{:S(2)}, u32[]{:S(2)}) %all-to-all-start) | async-done | bytes 6684704 | tf_op jit(solution)/shard_map/all_to_all | solution.py:71
  194.7 53.0 %all-gather.35.cloned.1.call-done = bf16[2048,1088]{0,1:T(8,128)(2,1)} async-done(((bf16[512,1088]{0,1:T(8,128)(2,1)}), bf16[2048,1088]{0,1:T(8,128)(2,1)}) %all-gather.35.cloned.1.call-update) | async-done | bytes 4456464 | tf_op jit(solution)/shard_map/all_gather | solution.py:118
  247.7 28.6 %fusion.2 = (f32[17,512]{1,0:T(8,128)S(1)}, f32[17,512,2048]{2,1,0:T(8,128)}) fusion(pred[512,2048]{1,0:T(8,128)(4,1)S(1)} %fusion.20, bf16[512,17,64]{0,2,1:T(8,128)(2,1)S(1)} %bitcast.144, bf16[2048,17,64]{0,2,1:T(8,128)(2,1)} %bitcast.138), kind=kOutput, calls=%fused_computation.10 | convolution fusion | flops 2335170048 | bytes 77957120 | tf_op jit(solution)/shard_map/while/body/eval_jaxpr/qhd,khd->hqk/dot_general | solution.py:102
  276.3 23.5 %fusion = f32[17,512]{1,0:T(8,128)S(1)} fusion(f32[17,512,2048]{2,1,0:T(8,128)} %get-tuple-element.145, f32[17,512]{1,0:T(8,128)S(1)} %get-tuple-element.144, pred[512,2048]{1,0:T(8,128)(4,1)S(1)} %fusion.20), kind=kLoop, calls=%fused_computation.8 | loop fusion | flops 71294464 | bytes 72421376 | tf_op jit(solution)/shard_map/while/body/eval_jaxpr/reduce_sum | solution.py:130
  304.2 29.2 %fusion.25 = bf16[17,64,512]{2,1,0:T(8,128)(2,1)} fusion(bf16[2048,17,64]{0,2,1:T(8,128)(2,1)} %bitcast.154, f32[17,512,2048]{2,1,0:T(8,128)} %get-tuple-element.145, f32[17,512]{1,0:T(8,128)S(1)} %fusion, f32[17,512]{1,0:T(8,128)S(1)} %get-tuple-element.144, pred[512,2048]{1,0:T(8,128)(4,1)S(1)} %fusion.20), kind=kOutput, calls=%fused_computation.68 | convolution fusion | flops 2371387392 | bytes 77991936 | tf_op jit(solution)/shard_map/while/body/eval_jaxpr/hqk,khd->qhd/dot_general | solution.py:132
  334.7 15.7 all_gather.49
  350.4 37.9 %all-gather.25.cloned.1.call-done = bf16[2048,1088]{0,1:T(8,128)(2,1)} async-done(((bf16[512,1088]{0,1:T(8,128)(2,1)}), bf16[2048,1088]{0,1:T(8,128)(2,1)}) %all-gather.25.cloned.1.call-update) | async-done | bytes 4456464 | tf_op jit(solution)/shard_map/all_gather | solution.py:67
  407.6 17.5 all-to-all-done.1
  445.2 23.1 %reduce.7 = bf16[557056]{0:T(1024)(128)(2,1)S(1)} reduce(bf16[1,557056]{1,0:T(2,128)(2,1)S(1)} %copy-done.19, bf16[]{:T(256)} %constant.137), dimensions={0}, to_apply=%param.31.reduce_sub_computation | reduce | bytes 2228226 | tf_op args[15]
  472.5 22.7 %all_to_all.152 = bf16[512,4,272]{0,2,1:T(8,128)(2,1)S(1)} all-to-all(bf16[512,4,272]{0,2,1:T(8,128)(2,1)S(1)} %copy.81), channel_id=1, replica_groups=mesh['tok'=8,'mdl'=4] {'mdl'}, dimensions={1} | all-to-all | bytes 2228224 | tf_op jit(solution)/shard_map/all_to_all | solution.py:75
  501.9 18.2 fusion.44
  536.7 175.2 %all_to_all.153 = f32[4,512,1088]{1,2,0:T(8,128)} all-to-all(f32[4,512,1088]{1,2,0:T(8,128)S(1)} %bitcast.135), channel_id=1, replica_groups=mesh['tok'=8,'mdl'=4] {'mdl'}, dimensions={0} | all-to-all | bytes 17825792 | tf_op jit(solution)/shard_map/all_to_all | solution.py:71
  721.2 209.5 %reduce-scatter.17.cloned.1.call-done = f32[512,4352]{1,0:T(8,128)} async-done(((f32[2048,4352]{1,0:T(8,128)}), f32[512,4352]{1,0:T(8,128)}) %reduce-scatter.17.cloned.1.call-update) | async-done | bytes 8912912 | tf_op jit(solution)/shard_map/reduce_scatter | solution.py:79
  930.7 14.3 fusion.35
  951.6 56.8 %all_to_all.154 = bf16[512,4,1088]{0,2,1:T(8,128)(2,1)} all-to-all(bf16[512,4,1088]{0,2,1:T(8,128)(2,1)} %bitcast.140), channel_id=1, replica_groups=mesh['tok'=8,'mdl'=4] {'mdl'}, dimensions={1} | all-to-all | bytes 8912896 | tf_op jit(solution)/shard_map/all_to_all | solution.py:75
  1027.4 22.9 %convert_reduce_fusion = f32[557056]{0:T(1024)} fusion(bf16[1,557056]{1,0:T(2,128)(2,1)S(1)} %copy-done.20), kind=kLoop, calls=%fused_computation.53 | loop fusion | flops 557056 | bytes 3342336 | tf_op jit(solution)/shard_map/convert_element_type | solution.py:58
  1055.2 61.0 %reduce-scatter.19.cloned.1.call-done = f32[512,1088]{0,1:T(8,128)} async-done(((f32[2048,1088]{0,1:T(8,128)}), f32[512,1088]{0,1:T(8,128)}) %reduce-scatter.19.cloned.1.call-update) | async-done | bytes 2228240 | tf_op jit(solution)/shard_map/reduce_scatter | solution.py:79
  1123.2 17.8 all_to_all.155
  1148.6 88.7 %reduce-scatter.21.cloned.1.call-done = f32[512,1088]{0,1:T(8,128)} async-done(((f32[2048,1088]{0,1:T(8,128)}), f32[512,1088]{0,1:T(8,128)}) %reduce-scatter.21.cloned.1.call-update) | async-done | bytes 2228240 | tf_op jit(solution)/shard_map/reduce_scatter | solution.py:79
  1263.6 31.8 %all-gather.37.cloned.1.call-done = bf16[2048,1088]{0,1:T(8,128)(2,1)} async-done(((bf16[512,1088]{0,1:T(8,128)(2,1)}), bf16[2048,1088]{0,1:T(8,128)(2,1)}) %all-gather.37.cloned.1.call-update) | async-done | bytes 4456464 | tf_op jit(solution)/shard_map/all_gather | solution.py:196
  1295.4 32.5 %fusion.46 = f32[17,2048,512]{2,1,0:T(8,128)} fusion(bf16[2048,17,64]{0,2,1:T(8,128)(2,1)} %bitcast.156, bf16[512,17,64]{0,2,1:T(8,128)(2,1)S(1)} %bitcast.146), kind=kOutput, calls=%fused_computation.98 | convolution fusion | flops 2281701376 | bytes 76873728 | tf_op jit(solution)/shard_map/while/body/eval_jaxpr/qhd,khd->hqk/dot_general | solution.py:218
  1333.9 130.9 %all-gather.31.cloned.1.call-done = bf16[2048,4352]{1,0:T(8,128)(2,1)} async-done(((bf16[512,4352]{1,0:T(8,128)(2,1)}), bf16[2048,4352]{1,0:T(8,128)(2,1)}) %all-gather.31.cloned.1.call-update) | async-done | bytes 17825808 | tf_op jit(solution)/shard_map/all_gather | solution.py:67
  1482.0 54.1 %multiply_reduce_fusion = (f32[17,512]{1,0:T(8,128)S(1)}, f32[17,512,2048]{2,1,0:T(8,128)}) fusion(f32[17,512,2048]{2,1,0:T(8,128)} %get-tuple-element.145, f32[17,512]{1,0:T(8,128)S(1)} %log_add_fusion, pred[512,2048]{1,0:T(8,128)(4,1)S(1)} %copy-done.1, bf16[512,17,64]{0,2,1:T(8,128)(2,1)S(1)} %bitcast.145, bf16[2048,17,64]{0,2,1:T(8,128)(2,1)} %bitcast.155), kind=kOutput, calls=%fused_computation.3 | convolution fusion | flops 2370821632 | bytes 149295104 | tf_op jit(solution)/shard_map/while/body/eval_jaxpr/qhd,khd->hqk/dot_general | solution.py:177
  1536.1 48.6 %bitcast_convert_fusion.1 = (bf16[512,17,64]{0,2,1:T(8,128)(2,1)S(1)}, f32[17,64,512]{2,1,0:T(8,128)}) fusion(bf16[2048,17,64]{0,2,1:T(8,128)(2,1)} %bitcast.139, f32[17,512,2048]{2,1,0:T(8,128)} %get-tuple-element.149, f32[17,512,2048]{2,1,0:T(8,128)} %get-tuple-element.145, f32[17,512]{1,0:T(8,128)S(1)} %get-tuple-element.148, ...), kind=kOutput, calls=%fused_computation.48 | convolution fusion | flops 2389770240 | bytes 151523328 | tf_op jit(solution)/shard_map/while/body/eval_jaxpr/hqk,khd->qhd/dot_general | solution.py:183
  1594.5 38.6 %multiply_convert_fusion.5 = bf16[17,64,512]{2,1,0:T(8,128)(2,1)} fusion(bf16[2048,17,64]{0,2,1:T(8,128)(2,1)} %bitcast.157, f32[17,2048,512]{2,1,0:T(8,128)} %fusion.46, f32[17,2048]{1,0:T(8,128)} %bitcast.183, f32[17,2048]{1,0:T(8,128)} %bitcast.181, pred[2048,512]{1,0:T(8,128)(4,1)} %fusion.21, bf16[2048,17,64]{0,2,1:T(8,128)(2,1)} %bitcast.186, ...), kind=kOutput, calls=%fused_computation.58 | convolution fusion | flops 4671471616 | bytes 83771392 | tf_op jit(solution)/shard_map/while/body/eval_jaxpr/hqk,qhd->khd/dot_general | solution.py:228
  1633.1 29.6 %bitcast_convert_fusion = (bf16[512,17,64]{0,2,1:T(8,128)(2,1)}, f32[17,64,512]{2,1,0:T(8,128)}) fusion(bf16[2048,17,64]{0,2,1:T(8,128)(2,1)} %bitcast.187, f32[17,2048,512]{2,1,0:T(8,128)} %fusion.46, f32[17,2048]{1,0:T(8,128)S(1)} %bitcast.182, pred[2048,512]{1,0:T(8,128)(4,1)S(1)} %copy-done.30), kind=kOutput, calls=%fused_computation.46 | convolution fusion | flops 2353561600 | bytes 80289792 | tf_op jit(solution)/shard_map/while/body/eval_jaxpr/hqk,qhd->khd/dot_general | solution.py:231
  1664.2 40.3 %all_to_all.156 = bf16[512,4,816]{0,2,1:T(8,128)(2,1)S(1)} all-to-all(bf16[512,4,816]{0,2,1:T(8,128)(2,1)S(1)} %bitcast.142), channel_id=1, replica_groups=mesh['tok'=8,'mdl'=4] {'mdl'}, dimensions={1} | all-to-all | bytes 6684672 | tf_op jit(solution)/shard_map/all_to_all | solution.py:75
  1790.4 72.5 %reduce-scatter.23.cloned.1.call-done = f32[512,1088]{0,1:T(8,128)} async-done(((f32[2048,1088]{0,1:T(8,128)}), f32[512,1088]{0,1:T(8,128)}) %reduce-scatter.23.cloned.1.call-update) | async-done | bytes 2228240 | tf_op jit(solution)/shard_map/reduce_scatter | solution.py:79
  1868.7 13.5 reshape.400
  1882.2 42.0 %all-reduce.3 = (f32[1088]{0:T(1024)}, f32[1088]{0:T(1024)}, f32[1088]{0:T(1024)}, f32[1088]{0:T(1024)}, f32[1088]{0:T(1024)}, /*index=5*/f32[1088]{0:T(1024)}, f32[1088]{0:T(1024)}, f32[4352]{0:T(1024)}, f32[1088]{0:T(1024)}) all-reduce(f32[1088]{0:T(1024)S(1)} %get-tuple-element.93, ...), channel_id=1, replica_groups=mesh['tok'=8,'mdl'=4] {'tok','mdl'}, use_global_device_ids=true, to_apply=%region_20.21 | all-reduce | flops 13056 | bytes 104448 | tf_op jit(solution)/shard_map/psum | solution.py:266
  (267 shorter events, 313.3 us)
Async XLA Ops:
  7.2 33.1 %all-gather.23.cloned.1.call-start = ((), (), s32[]{:S(2)}) async-start(), calls=%async_computation.17 | async-start | bytes 2193408 | tf_op jit(solution)/shard_map/all_gather | solution.py:60
  7.9 89.0 %all-gather.21.cloned.1.call-start = ((), (), s32[]{:S(2)}) async-start(), calls=%async_computation.16 | async-start | bytes 5570560 | tf_op jit(solution)/shard_map/all_gather | solution.py:67
  107.7 79.8 %all-to-all-start = ((f32[4,512,816]{1,2,0:T(8,128)}), f32[4,512,816]{1,2,0:T(8,128)}, u32[]{:S(2)}, u32[]{:S(2)}) async-start(f32[4,512,816]{1,2,0:T(8,128)} %bitcast.137), calls=%async_computation | async-start | bytes 13369344 | tf_op jit(solution)/shard_map/all_to_all | solution.py:71
  113.2 134.6 %all-gather.35.cloned.1.call-start = ((), (), s32[]{:S(2)}) async-start(), calls=%async_computation.27 | async-start | bytes 5570560 | tf_op jit(solution)/shard_map/all_gather | solution.py:118
  192.8 83.5 %copy-start.15 = (bf16[512,1088]{0,1:T(8,128)(2,1)}, bf16[512,1088]{0,1:T(8,128)(2,1)S(1)}, u32[]{:S(2)}) copy-start(bf16[512,1088]{0,1:T(8,128)(2,1)S(1)} %get-tuple-element.142) | copy-start | bytes 3342340
  192.8 111.4 %all-gather.33.cloned.1.call-start = ((), (), s32[]{:S(2)}) async-start(), calls=%async_computation.26 | async-start | bytes 5570560 | tf_op jit(solution)/shard_map/all_gather | solution.py:119
  194.7 109.5 %copy-start = (pred[512,2048]{1,0:T(8,128)(4,1)}, pred[512,2048]{1,0:T(8,128)(4,1)S(1)}, u32[]{:S(2)}) copy-start(pred[512,2048]{1,0:T(8,128)(4,1)S(1)} %fusion.20) | copy-start | bytes 3145732
  194.7 193.6 %all-gather.25.cloned.1.call-start = ((), (), s32[]{:S(2)}) async-start(), calls=%async_computation.18 | async-start | bytes 5570560 | tf_op jit(solution)/shard_map/all_gather | solution.py:67
  333.4 163.0 %all-gather.41.cloned.1.call-start = ((), (), s32[]{:S(2)}) async-start(), calls=%async_computation.30 | async-start | bytes 3133440 | tf_op jit(solution)/shard_map/all_gather | solution.py:63
  334.0 186.1 %all-gather.29.cloned.1.call-start = ((), (), s32[]{:S(2)}) async-start(), calls=%async_computation.20 | async-start | bytes 2820096 | tf_op jit(solution)/shard_map/all_gather | solution.py:62
  393.8 31.3 %all-to-all-start.1 = ((f32[4,512,272]{1,2,0:T(8,128)}), f32[4,512,272]{1,2,0:T(8,128)}, u32[]{:S(2)}, u32[]{:S(2)}) async-start(f32[4,512,272]{1,2,0:T(8,128)} %bitcast.149), calls=%async_computation.1 | async-start | bytes 4456448 | tf_op jit(solution)/shard_map/all_to_all | solution.py:71
  398.4 128.0 %all-gather.27.cloned.1.call-start = ((), (), s32[]{:S(2)}) async-start(), calls=%async_computation.19 | async-start | bytes 5570560 | tf_op jit(solution)/shard_map/all_gather | solution.py:67
  445.0 485.8 %reduce-scatter.17.cloned.1.call-start = ((), (), s32[]{:S(2)}) async-start(), calls=%async_computation.22 | async-start | bytes 44564480 | tf_op jit(solution)/shard_map/reduce_scatter | solution.py:79
  520.1 596.1 %reduce-scatter.19.cloned.1.call-start = ((), (), s32[]{:S(2)}) async-start(), calls=%async_computation.23 | async-start | bytes 11141120 | tf_op jit(solution)/shard_map/reduce_scatter | solution.py:79
  711.8 218.9 %copy-start.48 = (f32[4352]{0:T(1024)S(1)}, f32[4352]{0:T(1024)}, u32[]{:S(2)}) copy-start(f32[4352]{0:T(1024)} %param.28) | copy-start | bytes 52228
  1025.8 211.4 %reduce-scatter.21.cloned.1.call-start = ((), (), s32[]{:S(2)}) async-start(), calls=%async_computation.24 | async-start | bytes 11141120 | tf_op jit(solution)/shard_map/reduce_scatter | solution.py:79
  1053.0 67.0 %copy-start.8 = (f32[512,1088]{1,0:T(8,128)}, f32[512,1088]{1,0:T(8,128)S(1)}, u32[]{:S(2)}) copy-start(f32[512,1088]{1,0:T(8,128)S(1)} %reshape.403) | copy-start | bytes 6684676
  1147.2 148.2 %all-gather.37.cloned.1.call-start = ((), (), s32[]{:S(2)}) async-start(), calls=%async_computation.28 | async-start | bytes 5570560 | tf_op jit(solution)/shard_map/all_gather | solution.py:196
  1147.8 317.0 %all-gather.31.cloned.1.call-start = ((), (), s32[]{:S(2)}) async-start(), calls=%async_computation.21 | async-start | bytes 22282240 | tf_op jit(solution)/shard_map/all_gather | solution.py:67
  1148.5 445.9 %all-gather.39.cloned.1.call-start = ((), (), s32[]{:S(2)}) async-start(), calls=%async_computation.29 | async-start | bytes 5570560 | tf_op jit(solution)/shard_map/all_gather | solution.py:197
  1240.1 505.6 %reduce-scatter.31.cloned.1.call-start = ((), (), s32[]{:S(2)}) async-start(), calls=%async_computation.34 | async-start | bytes 2820096
  1250.3 497.2 %reduce-scatter.29.cloned.1.call-start = ((), (), s32[]{:S(2)}) async-start(), calls=%async_computation.33 | async-start | bytes 940032
  1328.0 136.8 %copy-start.24 = (bf16[4,34,8,512]{3,2,0,1:T(8,128)(2,1)S(1)}, bf16[4,34,8,512]{3,2,0,1:T(8,128)(2,1)}, u32[]{:S(2)}) copy-start(bf16[4,34,8,512]{3,2,0,1:T(8,128)(2,1)} %copy.98) | copy-start | bytes 3342340
  1333.8 448.4 %reduce-scatter.25.cloned.1.call-start = ((), (), s32[]{:S(2)}) async-start(), calls=%async_computation.31 | async-start | bytes 3760128
  1481.9 306.7 %reduce-scatter.27.cloned.1.call-start = ((), (), s32[]{:S(2)}) async-start(), calls=%async_computation.32 | async-start | bytes 2193408
  1536.1 58.3 %copy-start.25 = (bf16[512,1088]{0,1:T(8,128)(2,1)S(1)}, bf16[512,1088]{0,1:T(8,128)(2,1)}, u32[]{:S(2)}) copy-start(bf16[512,1088]{0,1:T(8,128)(2,1)} %get-tuple-element.143) | copy-start | bytes 3342340
  1723.3 28.3 %all-to-all-start.3 = ((f32[4,512,272]{1,2,0:T(8,128)}), f32[4,512,272]{1,2,0:T(8,128)}, u32[]{:S(2)}, u32[]{:S(2)}) async-start(f32[4,512,272]{1,2,0:T(8,128)} %bitcast.148), calls=%async_computation.3 | async-start | bytes 4456448 | tf_op jit(solution)/shard_map/all_to_all | solution.py:71
  1727.9 135.0 %reduce-scatter.23.cloned.1.call-start = ((), (), s32[]{:S(2)}) async-start(), calls=%async_computation.25 | async-start | bytes 11141120 | tf_op jit(solution)/shard_map/reduce_scatter | solution.py:79
  1782.2 80.7 %copy-start.4 = (f32[512,1088]{0,1:T(8,128)S(1)}, f32[512,1088]{0,1:T(8,128)}, u32[]{:S(2)}) copy-start(f32[512,1088]{0,1:T(8,128)} %copy-done.2) | copy-start | bytes 6684676
  1782.2 80.7 %copy-start.36 = (f32[1088]{0:T(1024)S(1)}, f32[1088]{0:T(1024)}, u32[]{:S(2)}) copy-start(f32[1088]{0:T(1024)} %param.18) | copy-start | bytes 13060
  1782.2 80.7 %copy-start.40 = (f32[512]{0:T(512)S(1)}, f32[512]{0:T(512)}, u32[]{:S(2)}) copy-start(f32[512]{0:T(512)} %copy-done.39) | copy-start | bytes 6148
  1782.2 80.6 %copy-start.47 = (f32[512]{0:T(512)S(1)}, f32[512]{0:T(512)}, u32[]{:S(2)}) copy-start(f32[512]{0:T(512)} %copy-done.46) | copy-start | bytes 6148
  (51 other events, 584.7 us)
Sparse Core Ops, SparseCore 0:
  9.7 30.5 all-gather.22
  42.7 54.2 all-gather.20
  193.0 54.7 all-gather.34
  249.4 54.7 all-gather.32
  333.5 54.7 all-gather.24
  389.8 35.2 all-gather.40
  426.8 31.7 all-gather.28
  461.0 65.3 all-gather.26
  529.6 401.0 reduce-scatter.16
  1026.0 90.1 reduce-scatter.18
  1147.3 89.8 reduce-scatter.20
  1239.1 56.3 all-gather.36
  1297.4 167.3 all-gather.30
  1467.2 54.7 all-gather.38
  1524.2 38.4 reduce-scatter.30
  1564.9 30.8 reduce-scatter.28
  1598.1 40.2 reduce-scatter.24
  1712.9 36.8 reduce-scatter.26
  1772.1 90.7 reduce-scatter.22
where the time goes:
time: 1940 us; the launch traced here: 1930 us
  waiting for transfers between devices  852 us (44%)
  blocking collectives  389 us (20%)
  matrix products  370 us (19%)
  other arithmetic  168 us (9%)
  local copies, waits for them, and re-layouts  121 us (6%)
    reduce_scatter x4, waiting for transfers between devices, project_back(): lax.psum_scatter(jnp.einsum('rc,ic->ri', grad_cols, column_weights[matrix...  432 us
    all_gather x4, waiting for transfers between devices, project(): gathered = lax.all_gather(inputs, 'mdl', axis=0, tiled=True)  232 us
    all_to_all x1, blocking collectives, project(): lax.all_to_all(partial_out, 'mdl', split_axis=0, concat_axis=1, tiled=True)  175 us
    all_to_all x4, blocking collectives, project_back(): lax.all_to_all(gradient, 'mdl', split_axis=1, concat_axis=0, tiled=True)  138 us
    all_to_all x3, waiting for transfers between devices, project(): lax.all_to_all(partial_out, 'mdl', split_axis=0, concat_axis=1, tiled=True)  94.2 us
    dot_general x1, matrix products, attend_back(): jnp.einsum('qhd,khd->hqk', grad_heads, value_heads, preferred_element_typ...  54.1 us
    all_gather x1, waiting for transfers between devices, body(): lax.all_gather(key_local, 'mdl', axis=1, tiled=True)  53 us
    dot_general x1, matrix products, attend_back(): jnp.einsum('hqk,khd->qhd', d_scores, key_heads, preferred_element_type=jn...  48.6 us
  transfers between devices with their start and end apart: 22, of which 15 were waited for; matrix products, arithmetic and copies ran while one was open for 27% of the time, Pallas kernels for 0%

commit v1 on v0

v1 whole, which is shorter than its diff:
```python
import functools
import jax
import jax.numpy as jnp
from jax import lax
from jax.experimental import pallas as pl
from jax.experimental.pallas import tpu as pltpu
from jax.sharding import PartitionSpec as P

SEQ = 2048
HEAD_DIM = 64
SCORE_SCALE = 0.125
MASKED = -1e30
BLOCK = 256
EDGE = 512


def spans_of(block_index):
    start = block_index * BLOCK
    stop = start + BLOCK
    if start < EDGE or stop > SEQ - EDGE:
        spans = [(0, start, True, False), (start, stop, True, True)]
    else:
        spans = [(0, EDGE, True, False), (EDGE, start, False, False), (start, stop, False, True)]
    return [span for span in spans if span[1] > span[0]]


def dot_rows(left, right):
    return lax.dot_general(left, right, (((1,), (1,)), ((), ())), preferred_element_type=jnp.float32)


def dot_plain(left, right):
    return jnp.dot(left, right, preferred_element_type=jnp.float32)


def dot_cols(left, right):
    return lax.dot_general(left, right, (((0,), (0,)), ((), ())), preferred_element_type=jnp.float32)


def mask_scores(raw, span, doc_q, doc_row_ref):
    low, high, by_doc, causal = span
    keep = None
    if by_doc:
        keep = doc_q == doc_row_ref[0, :, low:high]
    if causal:
        row_pos = lax.broadcasted_iota(jnp.int32, raw.shape, 0)
        col_pos = lax.broadcasted_iota(jnp.int32, raw.shape, 1)
        below = col_pos <= row_pos
        keep = below if keep is None else keep & below
    return raw if keep is None else jnp.where(keep, raw, MASKED)


def attend_kernel(heads, q_ref, k_ref, v_ref, doc_col_ref, doc_row_ref, o_ref, lse_ref, qs, ks, vs, os):
    head = pl.program_id(1)
    for index in range(heads):
        @pl.when(head == index)
        def _():
            cols = slice(index * HEAD_DIM, (index + 1) * HEAD_DIM)
            qs[...] = q_ref[0, :, cols] * jnp.bfloat16(SCORE_SCALE)
            ks[...] = k_ref[0, :, cols]
            vs[...] = v_ref[0, :, cols]

    for block_index in range(SEQ // BLOCK):
        rows = slice(block_index * BLOCK, (block_index + 1) * BLOCK)
        query = qs[rows, :]
        doc_q = doc_col_ref[0, rows, :]
        spans = spans_of(block_index)
        scores = [
            mask_scores(dot_rows(query, ks[span[0] : span[1], :]), span, doc_q, doc_row_ref)
            for span in spans
        ]
        top = functools.reduce(
            jnp.maximum, [jnp.max(part, axis=-1, keepdims=True) for part in scores]
        )
        parts = [jnp.exp(part - top) for part in scores]
        total = sum(jnp.sum(part, axis=-1, keepdims=True) for part in parts)
        mixed = sum(
            dot_plain(part.astype(jnp.bfloat16), vs[span[0] : span[1], :])
            for part, span in zip(parts, spans)
        )
        os[rows, :] = (mixed / total).astype(jnp.bfloat16)
        lse_ref[0, rows, :] = top + jnp.log(total)
    for index in range(heads):
        @pl.when(head == index)
        def _():
            o_ref[0, :, index * HEAD_DIM : (index + 1) * HEAD_DIM] = os[...]


def attend_back_kernel(
    heads, q_ref, k_ref, v_ref, o_ref, do_ref, lse_ref, doc_col_ref, doc_row_ref,
    dq_ref, dk_ref, dv_ref, qs, ks, vs, os, dos, dqs, dks, dvs,
):
    head = pl.program_id(1)
    for index in range(heads):
        @pl.when(head == index)
        def _():
            cols = slice(index * HEAD_DIM, (index + 1) * HEAD_DIM)
            qs[...] = q_ref[0, :, cols] * jnp.bfloat16(SCORE_SCALE)
            ks[...] = k_ref[0, :, cols]
            vs[...] = v_ref[0, :, cols]
            os[...] = o_ref[0, :, cols]
            dos[...] = do_ref[0, :, cols]

    for block_index in reversed(range(SEQ // BLOCK)):
        rows = slice(block_index * BLOCK, (block_index + 1) * BLOCK)
        query = qs[rows, :]
        grad = dos[rows, :]
        doc_q = doc_col_ref[0, rows, :]
        total = lse_ref[0, rows, :]
        centre = jnp.sum(
            grad.astype(jnp.float32) * os[rows, :].astype(jnp.float32), axis=-1, keepdims=True
        )
        d_query = None
        for span in spans_of(block_index):
            keys = slice(span[0], span[1])
            scores = mask_scores(dot_rows(query, ks[keys, :]), span, doc_q, doc_row_ref)
            probs = jnp.exp(scores - total)
            d_probs = dot_rows(grad, vs[keys, :])
            d_scores = (probs * (d_probs - centre)).astype(jnp.bfloat16)
            d_value = dot_cols(probs.astype(jnp.bfloat16), grad)
            d_key = dot_cols(d_scores, query)
            part = dot_plain(d_scores, ks[keys, :])
            d_query = part if d_query is None else d_query + part
            if block_index == SEQ // BLOCK - 1:
                dvs[keys, :] = d_value
                dks[keys, :] = d_key
            else:
                dvs[keys, :] += d_value
                dks[keys, :] += d_key
        dqs[rows, :] = (d_query * SCORE_SCALE).astype(jnp.bfloat16)
    for index in range(heads):
        @pl.when(head == index)
        def _():
            cols = slice(index * HEAD_DIM, (index + 1) * HEAD_DIM)
            dq_ref[0, :, cols] = dqs[...]
            dk_ref[0, :, cols] = dks[...].astype(jnp.bfloat16)
            dv_ref[0, :, cols] = dvs[...].astype(jnp.bfloat16)


VMEM_LIMIT = 48 * 1024 * 1024


def attention_forward(queries, keys, values, doc_col, doc_row):
    windows, _, width = queries.shape
    heads = width // HEAD_DIM
    whole = pl.BlockSpec((1, SEQ, width), lambda w, h: (w, 0, 0))
    stat = pl.BlockSpec((1, SEQ, 1), lambda w, h: (w * heads + h, 0, 0))
    return pl.pallas_call(
        functools.partial(attend_kernel, heads),
        grid=(windows, heads),
        in_specs=[
            whole, whole, whole,
            pl.BlockSpec((1, SEQ, 1), lambda w, h: (w, 0, 0)),
            pl.BlockSpec((1, 1, SEQ), lambda w, h: (w, 0, 0)),
        ],
        out_specs=[whole, stat],
        out_shape=[
            jax.ShapeDtypeStruct(queries.shape, jnp.bfloat16),
            jax.ShapeDtypeStruct((windows * heads, SEQ, 1), jnp.float32),
        ],
        scratch_shapes=[pltpu.VMEM((SEQ, HEAD_DIM), jnp.bfloat16)] * 4,
        compiler_params=pltpu.CompilerParams(vmem_limit_bytes=VMEM_LIMIT),
        cost_estimate=pl.CostEstimate(
            flops=windows * heads * SEQ * SEQ * HEAD_DIM * 8,
            bytes_accessed=windows * SEQ * width * 8,
            transcendentals=windows * heads * SEQ * SEQ // 2,
        ),
    )(queries, keys, values, doc_col, doc_row)


def attention_backward(queries, keys, values, mixed, grads, lse, doc_col, doc_row):
    windows, _, width = queries.shape
    heads = width // HEAD_DIM
    whole = pl.BlockSpec((1, SEQ, width), lambda w, h: (w, 0, 0))
    stat = pl.BlockSpec((1, SEQ, 1), lambda w, h: (w * heads + h, 0, 0))
    return pl.pallas_call(
        functools.partial(attend_back_kernel, heads),
        grid=(windows, heads),
        in_specs=[
            whole, whole, whole, whole, whole, stat,
            pl.BlockSpec((1, SEQ, 1), lambda w, h: (w, 0, 0)),
            pl.BlockSpec((1, 1, SEQ), lambda w, h: (w, 0, 0)),
        ],
        out_specs=[whole, whole, whole],
        out_shape=[jax.ShapeDtypeStruct(queries.shape, jnp.bfloat16)] * 3,
        scratch_shapes=[pltpu.VMEM((SEQ, HEAD_DIM), jnp.bfloat16)] * 6
        + [pltpu.VMEM((SEQ, HEAD_DIM), jnp.float32)] * 2,
        compiler_params=pltpu.CompilerParams(vmem_limit_bytes=VMEM_LIMIT),
        cost_estimate=pl.CostEstimate(
            flops=windows * heads * SEQ * SEQ * HEAD_DIM * 20,
            bytes_accessed=windows * SEQ * width * 16,
            transcendentals=windows * heads * SEQ * SEQ // 2,
        ),
    )(queries, keys, values, mixed, grads, lse, doc_col, doc_row)


D = 1088
HEADS = 17
EPSILON = 1e-05
GELU_A = 0.7978845608028654
GELU_B = 0.044715


def normalize(values, gain_vec, shift_vec):
    centered = values - jnp.mean(values, axis=-1, keepdims=True)
    inv_root = lax.rsqrt(jnp.mean(centered * centered, axis=-1, keepdims=True) + EPSILON)
    scaled = centered * inv_root
    return (scaled * gain_vec + shift_vec, scaled, inv_root)


def normalize_back(gradient, scaled, inv_root, gain_vec):
    weighted = gradient * gain_vec
    inner = (
        weighted
        - jnp.mean(weighted, axis=-1, keepdims=True)
        - scaled * jnp.mean(weighted * scaled, axis=-1, keepdims=True)
    )
    return (inv_root * inner, jnp.sum(gradient * scaled, axis=0), jnp.sum(gradient, axis=0))


def gather_weight(weight):
    rows = lax.all_gather(weight, "tok", axis=0, tiled=True)
    return lax.all_gather(rows, "mdl", axis=1, tiled=True)


def scatter_grad(grad):
    rows = lax.psum_scatter(grad.astype(jnp.bfloat16), "tok", scatter_dimension=0, tiled=True)
    return lax.psum_scatter(rows, "mdl", scatter_dimension=1, tiled=True).astype(jnp.float32)


def body(
    hidden_in, doc_ids, ln1_gain, ln1_bias, w_qkv, q_bias, v_bias, w_out, out_bias,
    ln2_gain, ln2_bias, w_fc1, fc1_bias, w_fc2, fc2_bias, cotangent,
):
    groups = lax.axis_size("mdl")
    windows = hidden_in.shape[0]
    piece_len = hidden_in.shape[1] // D
    row_total = windows * piece_len
    width = -(-HEADS // groups) * HEAD_DIM
    x = hidden_in.reshape(row_total, D).astype(jnp.float32)
    cot_low = cotangent.reshape(row_total, D)
    cot = cot_low.astype(jnp.float32)
    qkv_full = gather_weight(w_qkv)
    out_full = gather_weight(w_out)
    fc1_full = gather_weight(w_fc1)
    fc2_full = gather_weight(w_fc2)

    def to_heads(rows):
        padded = jnp.pad(rows, ((0, 0), (0, groups * width - D)))
        parts = padded.reshape(windows, piece_len, groups, width)
        swapped = lax.all_to_all(parts, "mdl", split_axis=2, concat_axis=1, tiled=True)
        return swapped.reshape(windows, groups * piece_len, width)

    def to_rows(parts):
        split = parts.reshape(windows, groups, piece_len, width)
        swapped = lax.all_to_all(split, "mdl", split_axis=1, concat_axis=3, tiled=True)
        return swapped.reshape(row_total, groups * width)[:, :D]

    doc_row = doc_ids.reshape(windows, 1, SEQ)
    doc_col = doc_ids.reshape(windows, SEQ, 1)

    first, scaled_one, inv_one = normalize(x, ln1_gain, ln1_bias)
    h1 = first.astype(jnp.bfloat16)
    q_rows = (dot_plain(h1, qkv_full[:, :D]) + q_bias).astype(jnp.bfloat16)
    k_rows = dot_plain(h1, qkv_full[:, D : 2 * D]).astype(jnp.bfloat16)
    v_rows = (dot_plain(h1, qkv_full[:, 2 * D :]) + v_bias).astype(jnp.bfloat16)
    q_heads, k_heads, v_heads = to_heads(q_rows), to_heads(k_rows), to_heads(v_rows)
    mixed, lse = attention_forward(q_heads, k_heads, v_heads, doc_col, doc_row)
    attn = to_rows(mixed)
    mid = x + dot_plain(attn, out_full) + out_bias
    second, scaled_two, inv_two = normalize(mid, ln2_gain, ln2_bias)
    h2 = second.astype(jnp.bfloat16)
    pre = dot_plain(h2, fc1_full) + fc1_bias
    tanh = jnp.tanh(GELU_A * (pre + GELU_B * pre * pre * pre))
    act = (0.5 * pre * (1.0 + tanh)).astype(jnp.bfloat16)
    slope = 0.5 * (1.0 + tanh) + 0.5 * pre * (1.0 - tanh * tanh) * GELU_A * (
        1.0 + 3.0 * GELU_B * pre * pre
    )
    result = mid + dot_plain(act, fc2_full) + fc2_bias

    grad_fc2 = scatter_grad(dot_cols(act, cot_low))
    d_pre = dot_rows(cot_low, fc2_full) * slope
    d_pre_low = d_pre.astype(jnp.bfloat16)
    grad_fc1 = scatter_grad(dot_cols(h2, d_pre_low))
    d_h2 = dot_rows(d_pre_low, fc1_full)
    d_norm, ln2_gain_grad, ln2_bias_grad = normalize_back(d_h2, scaled_two, inv_two, ln2_gain)
    d_mid = cot + d_norm
    d_mid_low = d_mid.astype(jnp.bfloat16)
    grad_out = scatter_grad(dot_cols(attn, d_mid_low))
    d_attn = dot_rows(d_mid_low, out_full).astype(jnp.bfloat16)
    dq, dk, dv = attention_backward(
        q_heads, k_heads, v_heads, mixed, to_heads(d_attn), lse, doc_col, doc_row
    )
    dq_rows, dk_rows, dv_rows = to_rows(dq), to_rows(dk), to_rows(dv)
    d_qkv = jnp.concatenate([dq_rows, dk_rows, dv_rows], axis=-1)
    grad_qkv = scatter_grad(dot_cols(h1, d_qkv))
    d_h1 = dot_rows(d_qkv, qkv_full)
    d_norm, ln1_gain_grad, ln1_bias_grad = normalize_back(d_h1, scaled_one, inv_one, ln1_gain)
    d_input = d_mid + d_norm
    sums = (
        ln1_gain_grad,
        ln1_bias_grad,
        jnp.sum(dq_rows.astype(jnp.float32), axis=0),
        jnp.sum(dv_rows.astype(jnp.float32), axis=0),
        jnp.sum(d_mid, axis=0),
        ln2_gain_grad,
        ln2_bias_grad,
        jnp.sum(d_pre, axis=0),
        jnp.sum(cot, axis=0),
    )
    flat = lax.psum(jnp.concatenate(sums), ("tok", "mdl"))
    cuts, place = [], 0
    for part in sums:
        cuts.append(flat[place : place + part.shape[0]])
        place += part.shape[0]
    return (
        result.astype(jnp.bfloat16).reshape(windows, piece_len * D),
        d_input.astype(jnp.bfloat16).reshape(windows, piece_len * D),
        grad_qkv,
        grad_out,
        grad_fc1,
        grad_fc2,
        *cuts,
    )


def solution(mesh):
    both, tok, none = P("tok", "mdl"), P("tok"), P()
    in_specs = (
        both, tok, none, none, both, none, none, both, none,
        none, none, both, none, both, none, both,
    )
    out_specs = (both,) * 6 + (none,) * 9
    return jax.shard_map(body, mesh=mesh, in_specs=in_specs, out_specs=out_specs, check_vma=False)
```

time: 1940 us -> 1130 us (0.58)
  blocking collectives: 389 us -> 57.5 us
  matrix products: 370 us -> 113 us
  waiting for transfers between devices: 852 us -> 644 us
  other arithmetic: 168 us -> 58.6 us
  Pallas kernels: 0 us -> 90.3 us
    all_to_all x5 -> x0, blocking collectives: 313 us -> none  [the longest x1 175 us: project(): lax.all_to_all(partial_out, 'mdl', split_axis=0, concat_axis=1, tiled=True)]
    dot_general x19 -> x14, matrix products: 370 us -> 113 us  [the longest x6 40.1 us: dot_plain(): return jnp.dot(left, right, preferred_element_type=jnp.float32)]
    reduce_scatter x4 -> x3, waiting for transfers between devices: 432 us -> 225 us  [scatter_grad(): lax.psum_scatter(grad.astype(jnp.bfloat16), 'tok', scatter_dimension=0, t...]
    all_gather x11 -> x7, waiting for transfers between devices: 322 us -> 226 us  [the longest x4 150 us: gather_weight(): return lax.all_gather(rows, 'mdl', axis=1, tiled=True)]
    pallas_call x0 -> x2, Pallas kernels: none -> 90.3 us  [the longest x1 58.2 us: attention_backward(): pl.pallas_call(functools.partial(attend_back_kernel, heads), grid=(window...]
    unnamed x23 -> x20, waiting for transfers between devices: 3.37 us -> 83.5 us
    reduce_sum x8 -> x3, other arithmetic: 51.5 us -> 3.61 us  [the longest x1 1.87 us: body(): jnp.sum(d_mid, axis=0)]
    all_to_all x16 -> x4, local copies, waits for them, and re-layouts: 51.8 us -> 7.28 us  [to_heads(): lax.all_to_all(parts, 'mdl', split_axis=2, concat_axis=1, tiled=True)]
  transfers between devices with their start and end apart: 22 -> 23, of which waited for: 15 -> 19; matrix products, arithmetic and copies ran while one was open for 27% -> 21% of each run, Pallas kernels for 0% -> 8%
where the time goes in v1:
time: 1130 us; the launch traced here: 1120 us
  waiting for transfers between devices  644 us (57%)
  matrix products  113 us (10%)
  local copies, waits for them, and re-layouts  108 us (10%)
  Pallas kernels  90.3 us (8%)
  other arithmetic  58.6 us (5%)
  blocking collectives  57.5 us (5%)
  starting transfers between devices  31.9 us (3%)
  between operations  15.7 us (1%)
    reduce_scatter x3, waiting for transfers between devices, scatter_grad(): lax.psum_scatter(grad.astype(jnp.bfloat16), 'tok', scatter_dimension=0, t...  225 us
    all_gather x4, waiting for transfers between devices, gather_weight(): return lax.all_gather(rows, 'mdl', axis=1, tiled=True)  150 us
    unnamed x20, waiting for transfers between devices  83.5 us
    all_gather x3, waiting for transfers between devices, gather_weight(): rows = lax.all_gather(weight, 'tok', axis=0, tiled=True)  75.6 us
    all_to_all x4, waiting for transfers between devices, to_heads(): lax.all_to_all(parts, 'mdl', split_axis=2, concat_axis=1, tiled=True)  67 us
    pallas_call x1, Pallas kernels, attention_backward(): pl.pallas_call(functools.partial(attend_back_kernel, heads), grid=(window...  58.2 us
    all_to_all x4, waiting for transfers between devices, to_rows(): lax.all_to_all(split, 'mdl', split_axis=1, concat_axis=3, tiled=True)  42.3 us
    dot_general x6, matrix products, dot_plain(): return jnp.dot(left, right, preferred_element_type=jnp.float32)  40.1 us
  transfers between devices with their start and end apart: 23, of which 19 were waited for; matrix products, arithmetic and copies ran while one was open for 21% of the time, Pallas kernels for 8%

profile of v1, /device:TPU:0, one launch (start us, length us, event | category | flops | bytes accessed | tf_op | source)
XLA Modules:
  0.0 1118.5 jit_solution(4668624059341701853)
XLA Ops:
  9.5 30.8 %all-gather.9.cloned.1.call-done = bf16[1088,816]{1,0:T(8,128)(2,1)} async-done(((bf16[136,816]{1,0:T(8,128)(2,1)}), bf16[1088,816]{1,0:T(8,128)(2,1)}) %all-gather.9.cloned.1.call-update) | async-done | bytes 1775632 | tf_op jit(solution)/shard_map/all_gather | solution.py:221
  44.3 18.9 %all_gather.26 = bf16[1088,272]{1,0:T(8,128)(2,1)S(1)} all-gather(bf16[136,272]{1,0:T(8,128)(2,1)S(1)} %copy-done.26), channel_id=1, replica_groups=mesh['tok'=8,'mdl'=4] {'tok'}, dimensions={0}, use_global_device_ids=true | all-gather | bytes 665856 | tf_op jit(solution)/shard_map/all_gather | solution.py:221
  64.4 13.1 %all-gather.15.cloned.1.call-done = bf16[1088,1088]{1,0:T(8,128)(2,1)} async-done(((bf16[136,1088]{1,0:T(8,128)(2,1)}), bf16[1088,1088]{1,0:T(8,128)(2,1)}) %all-gather.15.cloned.1.call-update) | async-done | bytes 2367504 | tf_op jit(solution)/shard_map/all_gather | solution.py:221
  82.7 31.6 %all-gather.21.cloned.1.call-done = bf16[8,544,272]{1,2,0:T(8,128)(2,1)} async-done(((bf16[1,544,272]{1,2,0:T(8,128)(2,1)}), bf16[8,544,272]{1,2,0:T(8,128)(2,1)}) %all-gather.21.cloned.1.call-update) | async-done | bytes 2367504 | tf_op jit(solution)/shard_map/all_gather | solution.py:221
  119.8 21.9 %convert_reduce_fusion.1 = f32[557056]{0:T(1024)S(1)} fusion(bf16[1,557056]{1,0:T(2,128)(2,1)} %param.16), kind=kLoop, calls=%fused_computation.30 | loop fusion | flops 557056 | bytes 3342336 | tf_op jit(solution)/shard_map/convert_element_type | solution.py:239
  149.8 46.2 %all-gather.11.cloned.1.call-done = bf16[1088,3264]{0,1:T(8,128)(2,1)} async-done(((bf16[1088,816]{0,1:T(8,128)(2,1)}), bf16[1088,3264]{0,1:T(8,128)(2,1)}) %all-gather.11.cloned.1.call-update) | async-done | bytes 7102480 | tf_op jit(solution)/shard_map/all_gather | solution.py:222
  208.8 18.7 %all-to-all-done = bf16[1,512,4,320]{1,3,0,2:T(8,128)(2,1)S(1)} async-done(((bf16[1,512,4,320]{1,3,0,2:T(8,128)(2,1)}), bf16[1,512,4,320]{1,3,0,2:T(8,128)(2,1)S(1)}, u32[]{:S(2)}, u32[]{:S(2)}) %all-to-all-start) | async-done | bytes 1310752 | tf_op jit(solution)/shard_map/all_to_all | solution.py:250
  236.2 24.4 %all-to-all-done.1 = bf16[1,512,4,320]{1,3,0,2:T(8,128)(2,1)S(1)} async-done(((bf16[1,512,4,320]{1,3,0,2:T(8,128)(2,1)}), bf16[1,512,4,320]{1,3,0,2:T(8,128)(2,1)S(1)}, u32[]{:S(2)}, u32[]{:S(2)}) %all-to-all-start.1) | async-done | bytes 1310752 | tf_op jit(solution)/shard_map/all_to_all | solution.py:250
  269.6 11.6 %all-to-all-done.2 = bf16[1,512,4,320]{1,3,0,2:T(8,128)(2,1)} async-done(((bf16[1,512,4,320]{1,3,0,2:T(8,128)(2,1)}), bf16[1,512,4,320]{1,3,0,2:T(8,128)(2,1)}, u32[]{:S(2)}, u32[]{:S(2)}) %all-to-all-start.2) | async-done | bytes 1310752 | tf_op jit(solution)/shard_map/all_to_all | solution.py:250
  285.0 32.1 %shard_map.271 = (bf16[1,2048,320]{2,1,0:T(8,128)(2,1)S(1)}, f32[5,2048,1]{2,1,0:T(8,128)}) custom-call(bf16[1,2048,320]{2,1,0:T(8,128)(2,1)S(1)} %bitcast.82, bf16[1,2048,320]{2,1,0:T(8,128)(2,1)S(1)} %bitcast.84, bf16[1,2048,320]{2,1,0:T(8,128)(2,1)} %bitcast.105, s32[1,2048,1]{2,1,0:T(8,128)S(1)} %copy-done.4, s32[1,1,2048]{2,1,0:T(1,128)S(1)} %bitcast.91), custom_call_target="tpu_custom_call" | custom-call | flops 10737418240 | bytes 5242880 | tf_op jit(solution)/shard_map/pallas_call | solution.py:147
  325.6 24.1 %reduce.1 = bf16[557056]{0:T(1024)(128)(2,1)} reduce(bf16[1,557056]{1,0:T(2,128)(2,1)S(1)} %copy-done.20, bf16[]{:T(256)} %constant.46), dimensions={0}, to_apply=%param.31.reduce_sub_computation | reduce | bytes 2228226 | tf_op args[15]
  360.5 19.3 %all-gather.17.cloned.1.call-done = bf16[1088,4352]{0,1:T(8,128)(2,1)} async-done(((bf16[1088,1088]{0,1:T(8,128)(2,1)}), bf16[1088,4352]{0,1:T(8,128)(2,1)}) %all-gather.17.cloned.1.call-update) | async-done | bytes 9469968 | tf_op jit(solution)/shard_map/all_gather | solution.py:222
  379.8 13.4 %fusion.24 = f32[512,4352]{1,0:T(8,128)} fusion(bf16[1088,4352]{0,1:T(8,128)(2,1)} %all-gather.17.cloned.1.call-done, f32[512,1088]{0,1:T(8,128)} %copy-done.12, f32[1088]{0:T(1024)S(1)} %copy-done.51, f32[1088]{0:T(1024)S(1)} %copy-done.42, f32[512]{0:T(512)S(1)} %add_rsqrt_fusion, f32[512]{0:T(512)S(1)} %broadcast_multiply_fusion.4), kind=kOutput, calls=%fused_computation.65 | convolution fusion | flops 4851400704 | bytes 20623872 | tf_op jit(solution)/shard_map/dot_general | solution.py:32
  393.2 85.0 %all-gather.19.cloned.1.call-done = bf16[4352,1088]{0,1:T(8,128)(2,1)} async-done(((bf16[4352,272]{0,1:T(8,128)(2,1)}), bf16[4352,1088]{0,1:T(8,128)(2,1)}) %all-gather.19.cloned.1.call-update) | async-done | bytes 9469968 | tf_op jit(solution)/shard_map/all_gather | solution.py:222
  478.2 16.9 %fusion.28 = (f32[4352]{0:T(1024)}, bf16[512,4352]{1,0:T(8,128)(2,1)}) fusion(f32[512,4352]{1,0:T(8,128)} %fusion.24, f32[4352]{0:T(1024)S(1)} %copy-done.46, bf16[512,1088]{1,0:T(8,128)(2,1)S(1)} %reshape.168, bf16[4352,1088]{0,1:T(8,128)(2,1)} %all-gather.19.cloned.1.call-done), kind=kOutput, calls=%fused_computation.69 | convolution fusion | flops 4895404032 | bytes 23988224 | tf_op jit(solution)/shard_map/dot_general | solution.py:28
  495.1 10.8 multiply_reduce_fusion
  518.6 12.2 %all-to-all-done.4 = bf16[1,512,4,320]{1,3,0,2:T(8,128)(2,1)S(1)} async-done(((bf16[1,512,4,320]{1,3,0,2:T(8,128)(2,1)}), bf16[1,512,4,320]{1,3,0,2:T(8,128)(2,1)S(1)}, u32[]{:S(2)}, u32[]{:S(2)}) %all-to-all-start.4) | async-done | bytes 1310752 | tf_op jit(solution)/shard_map/all_to_all | solution.py:250
  533.7 58.2 %shard_map.272 = (bf16[1,2048,320]{2,1,0:T(8,128)(2,1)S(1)}, bf16[1,2048,320]{2,1,0:T(8,128)(2,1)S(1)}, bf16[1,2048,320]{2,1,0:T(8,128)(2,1)S(1)}) custom-call(bf16[1,2048,320]{2,1,0:T(8,128)(2,1)} %bitcast.83, bf16[1,2048,320]{2,1,0:T(8,128)(2,1)} %bitcast.85, bf16[1,2048,320]{2,1,0:T(8,128)(2,1)} %bitcast.106, bf16[1,2048,320]{2,1,0:T(8,128)(2,1)} %copy-done.2, ...), custom_call_target="tpu_custom_call" | custom-call | flops 26843545600 | bytes 10485760 | tf_op jit(solution)/shard_map/pallas_call | solution.py:175
  601.5 14.4 %all-to-all-done.7 = bf16[1,4,512,320]{2,3,0,1:T(8,128)(2,1)} async-done(((bf16[1,4,512,320]{2,3,0,1:T(8,128)(2,1)}), bf16[1,4,512,320]{2,3,0,1:T(8,128)(2,1)}, u32[]{:S(2)}, u32[]{:S(2)}) %all-to-all-start.7) | async-done | bytes 1310752 | tf_op jit(solution)/shard_map/all_to_all | solution.py:255
  621.0 14.3 %all-to-all-done.6 = bf16[1,4,512,320]{2,3,0,1:T(8,128)(2,1)S(1)} async-done(((bf16[1,4,512,320]{2,3,0,1:T(8,128)(2,1)}), bf16[1,4,512,320]{2,3,0,1:T(8,128)(2,1)S(1)}, u32[]{:S(2)}, u32[]{:S(2)}) %all-to-all-start.6) | async-done | bytes 1310752 | tf_op jit(solution)/shard_map/all_to_all | solution.py:255
  642.3 12.3 %all-to-all-done.5 = bf16[1,4,512,320]{2,3,0,1:T(8,128)(2,1)S(1)} async-done(((bf16[1,4,512,320]{2,3,0,1:T(8,128)(2,1)}), bf16[1,4,512,320]{2,3,0,1:T(8,128)(2,1)S(1)}, u32[]{:S(2)}, u32[]{:S(2)}) %all-to-all-start.5) | async-done | bytes 1310752 | tf_op jit(solution)/shard_map/all_to_all | solution.py:255
  664.2 12.2 %convolution_convert_fusion = bf16[4352,1088]{1,0:T(8,128)(2,1)} fusion(bf16[512,1088]{1,0:T(8,128)(2,1)S(1)} %copy-done.18, f32[512,4352]{1,0:T(8,128)} %fusion.24, f32[4352]{0:T(1024)S(1)} %copy-done.47), kind=kOutput, calls=%fused_computation | convolution fusion | flops 4875632640 | bytes 19514368 | tf_op jit(solution)/shard_map/dot_general | solution.py:36
  678.0 10.1 convolution_convert_fusion.1
  690.3 51.9 %reduce-scatter.17.cloned.1.call-done = bf16[136,3264]{1,0:T(8,128)(2,1)} async-done(((bf16[1088,3264]{1,0:T(8,128)(2,1)}), bf16[136,3264]{1,0:T(8,128)(2,1)}) %reduce-scatter.17.cloned.1.call-update) | async-done | bytes 887824 | tf_op jit(solution)/shard_map/reduce_scatter | solution.py:226
  746.8 101.1 %reduce-scatter.21.cloned.1.call-done = bf16[544,1088]{1,0:T(8,128)(2,1)} async-done(((bf16[4352,1088]{1,0:T(8,128)(2,1)}), bf16[544,1088]{1,0:T(8,128)(2,1)}) %reduce-scatter.21.cloned.1.call-update) | async-done | bytes 1183760 | tf_op jit(solution)/shard_map/reduce_scatter | solution.py:226
  847.9 12.5 %fusion.8 = bf16[512,1088]{0,1:T(8,128)(2,1)} fusion(f32[512,1088]{0,1:T(8,128)S(1)} %copy-done.15, bf16[4352,1088]{0,1:T(8,128)(2,1)} %all-gather.19.cloned.1.call-done, f32[1088]{0:T(1024)S(1)} %copy-done.52, f32[512,4352]{1,0:T(8,128)} %fusion.24, f32[4352]{0:T(1024)} %param.28), kind=kOutput, calls=%fused_computation.20 | convolution fusion | flops 4872568832 | bytes 21746944 | tf_op jit(solution)/shard_map/dot_general | solution.py:32
  864.6 12.1 %reshape.167 = bf16[1,557056]{1,0:T(2,128)(2,1)} reshape(bf16[557056]{0:T(1024)(128)(2,1)} %reshape.199) | data formatting | bytes 2228224 | tf_op jit(solution)/shard_map/reshape | solution.py:316
  876.7 71.9 %reduce-scatter.19.cloned.1.call-done = bf16[136,4352]{1,0:T(8,128)(2,1)} async-done(((bf16[1088,4352]{1,0:T(8,128)(2,1)}), bf16[136,4352]{1,0:T(8,128)(2,1)}) %reduce-scatter.19.cloned.1.call-update) | async-done | bytes 1183760 | tf_op jit(solution)/shard_map/reduce_scatter | solution.py:226
  967.6 12.4 %reshape.177 = bf16[1,557056]{1,0:T(2,128)(2,1)} reshape(bf16[557056]{0:T(1024)(128)(2,1)} %reshape.201) | data formatting | bytes 2228224 | tf_op jit(solution)/shard_map/reshape | solution.py:317
  981.9 38.6 %psum.7 = f32[13056]{0:T(1024)S(1)} all-reduce(f32[13056]{0:T(1024)S(1)} %concatenate.7), channel_id=1, replica_groups=mesh['tok'=8,'mdl'=4] {'tok','mdl'}, use_global_device_ids=true, to_apply=%region_25.26 | all-reduce | flops 13056 | bytes 104448 | tf_op jit(solution)/shard_map/psum | solution.py:310
  1025.7 44.2 %all-reduce.8.cloned.1.call-done = bf16[544,1088]{1,0:T(8,128)(2,1)} async-done(((bf16[544,1088]{1,0:T(8,128)(2,1)}), bf16[544,1088]{1,0:T(8,128)(2,1)}) %all-reduce.8.cloned.1.call-update) | async-done | bytes 1183760
  1072.3 37.0 %reduce-scatter.27.cloned.1.call-done = bf16[1088,136]{1,0:T(8,128)(2,1)} async-done(((bf16[4352,136]{1,0:T(8,128)(2,1)}), bf16[1088,136]{1,0:T(8,128)(2,1)}) %reduce-scatter.27.cloned.1.call-update) | async-done | bytes 295952
  (216 shorter events, 168.3 us)
Async XLA Ops:
  7.2 33.1 %all-gather.9.cloned.1.call-start = ((), (), s32[]{:S(2)}) async-start(), calls=%async_computation.15 | async-start | bytes 2193408 | tf_op jit(solution)/shard_map/all_gather | solution.py:221
  7.9 69.6 %all-gather.15.cloned.1.call-start = ((), (), s32[]{:S(2)}) async-start(), calls=%async_computation.18 | async-start | bytes 2820096 | tf_op jit(solution)/shard_map/all_gather | solution.py:221
  8.7 105.7 %all-gather.21.cloned.1.call-start = ((), (), s32[]{:S(2)}) async-start(), calls=%async_computation.24 | async-start | bytes 3133440 | tf_op jit(solution)/shard_map/all_gather | solution.py:221
  9.4 186.6 %all-gather.11.cloned.1.call-start = ((), (), s32[]{:S(2)}) async-start(), calls=%async_computation.16 | async-start | bytes 9400320 | tf_op jit(solution)/shard_map/all_gather | solution.py:222
  44.2 309.7 %all-gather.13.cloned.1.call-start = ((), (), s32[]{:S(2)}) async-start(), calls=%async_computation.17 | async-start | bytes 3133440 | tf_op jit(solution)/shard_map/all_gather | solution.py:222
  64.3 315.4 %all-gather.17.cloned.1.call-start = ((), (), s32[]{:S(2)}) async-start(), calls=%async_computation.19 | async-start | bytes 12533760 | tf_op jit(solution)/shard_map/all_gather | solution.py:222
  82.7 395.6 %all-gather.19.cloned.1.call-start = ((), (), s32[]{:S(2)}) async-start(), calls=%async_computation.20 | async-start | bytes 11837440 | tf_op jit(solution)/shard_map/all_gather | solution.py:222
  149.8 49.5 %copy-start.21 = (bf16[512,1088]{0,1:T(8,128)(2,1)}, bf16[512,1088]{0,1:T(8,128)(2,1)S(1)}, u32[]{:S(2)}) copy-start(bf16[512,1088]{0,1:T(8,128)(2,1)S(1)} %add_convert_fusion.2) | copy-start | bytes 3342340
  200.4 27.1 %all-to-all-start = ((bf16[1,512,4,320]{1,3,0,2:T(8,128)(2,1)}), bf16[1,512,4,320]{1,3,0,2:T(8,128)(2,1)S(1)}, u32[]{:S(2)}, u32[]{:S(2)}) async-start(bf16[1,512,4,320]{1,3,0,2:T(8,128)(2,1)} %bitcast.1), calls=%async_computation | async-start | bytes 2621440 | tf_op jit(solution)/shard_map/all_to_all | solution.py:250
  227.5 33.1 %all-to-all-start.1 = ((bf16[1,512,4,320]{1,3,0,2:T(8,128)(2,1)}), bf16[1,512,4,320]{1,3,0,2:T(8,128)(2,1)S(1)}, u32[]{:S(2)}, u32[]{:S(2)}) async-start(bf16[1,512,4,320]{1,3,0,2:T(8,128)(2,1)} %bitcast.102), calls=%async_computation.1 | async-start | bytes 2621440 | tf_op jit(solution)/shard_map/all_to_all | solution.py:250
  260.7 20.5 %all-to-all-start.2 = ((bf16[1,512,4,320]{1,3,0,2:T(8,128)(2,1)}), bf16[1,512,4,320]{1,3,0,2:T(8,128)(2,1)}, u32[]{:S(2)}, u32[]{:S(2)}) async-start(bf16[1,512,4,320]{1,3,0,2:T(8,128)(2,1)} %bitcast.101), calls=%async_computation.2 | async-start | bytes 2621440 | tf_op jit(solution)/shard_map/all_to_all | solution.py:250
  320.9 34.2 %all-to-all-start.3 = ((bf16[1,4,512,320]{2,3,0,1:T(8,128)(2,1)}), bf16[1,4,512,320]{2,3,0,1:T(8,128)(2,1)}, u32[]{:S(2)}, u32[]{:S(2)}) async-start(bf16[1,4,512,320]{2,3,0,1:T(8,128)(2,1)} %copy.86), calls=%async_computation.3 | async-start | bytes 2621440 | tf_op jit(solution)/shard_map/all_to_all | solution.py:255
  352.4 125.8 %copy-start.17 = (bf16[512,1088]{1,0:T(8,128)(2,1)}, bf16[512,1088]{1,0:T(8,128)(2,1)S(1)}, u32[]{:S(2)}) copy-start(bf16[512,1088]{1,0:T(8,128)(2,1)S(1)} %reshape.168) | copy-start | bytes 3342340
  358.8 147.1 %copy-start.35 = (f32[512]{0:T(512)}, f32[512]{0:T(512)S(1)}, u32[]{:S(2)}) copy-start(f32[512]{0:T(512)S(1)} %broadcast_multiply_fusion.4) | copy-start | bytes 6148
  360.5 145.5 %copy-start.43 = (f32[512]{0:T(512)}, f32[512]{0:T(512)S(1)}, u32[]{:S(2)}) copy-start(f32[512]{0:T(512)S(1)} %add_rsqrt_fusion) | copy-start | bytes 6148
  360.5 117.8 %copy-start.46 = (f32[4352]{0:T(1024)S(1)}, f32[4352]{0:T(1024)}, u32[]{:S(2)}) copy-start(f32[4352]{0:T(1024)} %param.28) | copy-start | bytes 52228
  393.2 101.9 %copy-start.13 = (f32[512,1088]{0,1:T(8,128)S(1)}, f32[512,1088]{0,1:T(8,128)}, u32[]{:S(2)}) copy-start(f32[512,1088]{0,1:T(8,128)} %copy-done.12) | copy-start | bytes 6684676
  510.7 20.2 %all-to-all-start.4 = ((bf16[1,512,4,320]{1,3,0,2:T(8,128)(2,1)}), bf16[1,512,4,320]{1,3,0,2:T(8,128)(2,1)S(1)}, u32[]{:S(2)}, u32[]{:S(2)}) async-start(bf16[1,512,4,320]{1,3,0,2:T(8,128)(2,1)} %bitcast.100), calls=%async_computation.4 | async-start | bytes 2621440 | tf_op jit(solution)/shard_map/all_to_all | solution.py:250
  514.2 174.0 %reduce-scatter.29.cloned.1.call-start = ((), (), s32[]{:S(2)}) async-start(), calls=%async_computation.29 | async-start | bytes 2820096
  595.6 20.3 %all-to-all-start.7 = ((bf16[1,4,512,320]{2,3,0,1:T(8,128)(2,1)}), bf16[1,4,512,320]{2,3,0,1:T(8,128)(2,1)}, u32[]{:S(2)}, u32[]{:S(2)}) async-start(bf16[1,4,512,320]{2,3,0,1:T(8,128)(2,1)} %copy.98), calls=%async_computation.7 | async-start | bytes 2621440 | tf_op jit(solution)/shard_map/all_to_all | solution.py:255
  615.9 19.4 %all-to-all-start.6 = ((bf16[1,4,512,320]{2,3,0,1:T(8,128)(2,1)}), bf16[1,4,512,320]{2,3,0,1:T(8,128)(2,1)S(1)}, u32[]{:S(2)}, u32[]{:S(2)}) async-start(bf16[1,4,512,320]{2,3,0,1:T(8,128)(2,1)} %copy.97), calls=%async_computation.6 | async-start | bytes 2621440 | tf_op jit(solution)/shard_map/all_to_all | solution.py:255
  635.3 19.4 %all-to-all-start.5 = ((bf16[1,4,512,320]{2,3,0,1:T(8,128)(2,1)}), bf16[1,4,512,320]{2,3,0,1:T(8,128)(2,1)S(1)}, u32[]{:S(2)}, u32[]{:S(2)}) async-start(bf16[1,4,512,320]{2,3,0,1:T(8,128)(2,1)} %copy.96), calls=%async_computation.5 | async-start | bytes 2621440 | tf_op jit(solution)/shard_map/all_to_all | solution.py:255
  638.8 103.4 %reduce-scatter.17.cloned.1.call-start = ((), (), s32[]{:S(2)}) async-start(), calls=%async_computation.21 | async-start | bytes 8146944 | tf_op jit(solution)/shard_map/reduce_scatter | solution.py:226
  663.0 184.9 %reduce-scatter.21.cloned.1.call-start = ((), (), s32[]{:S(2)}) async-start(), calls=%async_computation.23 | async-start | bytes 11280384 | tf_op jit(solution)/shard_map/reduce_scatter | solution.py:226
  676.4 272.2 %reduce-scatter.19.cloned.1.call-start = ((), (), s32[]{:S(2)}) async-start(), calls=%async_computation.22 | async-start | bytes 10653696 | tf_op jit(solution)/shard_map/reduce_scatter | solution.py:226
  688.1 333.8 %reduce-scatter.25.cloned.1.call-start = ((), (), s32[]{:S(2)}) async-start(), calls=%async_computation.26 | async-start | bytes 696320
  690.2 157.7 %copy-start.52 = (f32[1088]{0:T(1024)S(1)}, f32[1088]{0:T(1024)}, u32[]{:S(2)}) copy-start(f32[1088]{0:T(1024)} %param.30) | copy-start | bytes 13060
  690.2 333.4 %reduce-scatter.23.cloned.1.call-start = ((), (), s32[]{:S(2)}) async-start(), calls=%async_computation.25 | async-start | bytes 2088960
  744.8 325.1 %all-reduce.8.cloned.1.call-start = ((), (), s32[]{:S(2)}) async-start(), calls=%async_computation.28 | async-start | bytes 2506752
  847.9 261.4 %reduce-scatter.27.cloned.1.call-start = ((), (), s32[]{:S(2)}) async-start(), calls=%async_computation.27 | async-start | bytes 2785280
  876.7 75.6 %copy-start.9 = (f32[512,1088]{0,1:T(8,128)S(1)}, f32[512,1088]{0,1:T(8,128)}, u32[]{:S(2)}) copy-start(f32[512,1088]{0,1:T(8,128)} %copy-done.7) | copy-start | bytes 6684676
  876.7 75.6 %copy-start.28 = (f32[1088]{0:T(1024)S(1)}, f32[1088]{0:T(1024)}, u32[]{:S(2)}) copy-start(f32[1088]{0:T(1024)} %param.18) | copy-start | bytes 13060
  (44 other events, 466.6 us)
Sparse Core Ops, SparseCore 0:
  9.7 30.5 all-gather.8
  41.9 35.5 all-gather.14
  79.1 35.1 all-gather.20
  116.6 79.2 all-gather.10
  198.2 62.6 all-gather.12
  262.7 117.0 all-gather.16
  381.6 96.5 all-gather.18
  518.8 39.8 reduce-scatter.28
  663.1 79.0 reduce-scatter.16
  744.4 103.4 reduce-scatter.20
  850.2 98.4 reduce-scatter.18
  951.9 23.2 reduce-scatter.24
  978.6 32.1 reduce-scatter.22
  1014.1 55.7 all-reduce.7
  1072.8 36.5 reduce-scatter.26
